TPU v7x, 512 devices: a whole 4x4x16 slice. The times are simulated.
512 devices in a mesh: areal: 32 (over y, x, core), layer: 16 (over z).
Axes of the slice: x: 4, y: 4, z: 16, core: 2. Of those that a mesh axis runs over, the one named last changes fastest.
Arguments:
- rhs: bfloat16 [32, 32, 112, 384], P('areal', 'layer'), may hold values from -6 to 6
- areal_blocks: bfloat16 [32, 32, 6, 384, 384], P('areal', 'layer'), may hold values from -0.078125 to 0.078125
- vertical_blocks: bfloat16 [32, 32, 2, 384, 384], P('areal', 'layer'), may hold values from -0.078125 to 0.078125
- conn_src: int32 [32, 16, 6], P('areal', 'layer'), may hold values from 0 to 63, as said below
- conn_count: int32 [32, 16], P('areal', 'layer'), may hold values from 1 to 6, as said below
- tile_map: int32 [64], replicated, may hold values from 0 to 63, as said below
- well_cells: int32 [32, 32, 4], P('areal', 'layer'), may hold values from 0 to 127
- well_gain: float32 [32, 32, 4], P('areal', 'layer'), may hold values from -24 to 24
- sens: float32 [32, 32, 3, 128], P('areal', 'layer'), may hold values from -6 to 6
- basis: bfloat16 [32, 32, 128, 256], P('areal', 'layer'), may hold values from -0.015625 to 0.015625
Outputs:
- adjoint: bfloat16 [32, 32, 112, 384], P('areal', 'layer')
- coefficients: bfloat16 [112, 256], P('layer', 'areal')
Inputs may be any that keep to these rules, and one draw needn't show every extreme that they name: Tile t of a layer group's plane is held by device column tile_map[t] // 2 in tile layer 2 g + tile_map[t] % 2; each value is held by one tile. `conn_src`: the 6 sources of device column c lie, in some order, on the 6 device columns (c + k) mod 32 with k one of 1 to 2, their negatives, 16 and 17, one on each. `conn_count`: the live connections of a device are its first ones. `well_cells`: cells of a tile, repeats allowed.
All inputs are finite; a program needn't handle non-finite values.
Results may differ from a plain program's by a relative error of at most 0.02.
Values may be sent and summed in bfloat16 or wider, within the bound.
A program may use at most 64 MiB of HBM per device.

v0:
```python
import jax
import jax.numpy as jnp
from jax import lax
from jax.sharding import PartitionSpec as P

ITERS = 3


def extended(x, sides, width):
    for axis, dim in sides:
        size, length = (lax.axis_size(axis), x.shape[dim])
        up = [(i, (i + 1) % size) for i in range(size - 1)]
        down = [(j, i) for i, j in up]
        last = lax.slice_in_dim(x, length - width, length, axis=dim)
        leading = lax.slice_in_dim(x, 0, width, axis=dim)
        before = lax.ppermute(last, axis, up)
        after = lax.ppermute(leading, axis, down)
        x = jnp.concatenate([before, x, after], axis=dim)
    return x


def on_device(
    rhs,
    areal_blocks,
    vertical_blocks,
    conn_src,
    conn_count,
    tile_map,
    well_cells,
    well_gain,
    sens,
    basis,
):
    cells = sens.shape[-1]
    phases = sens.shape[-2]
    rows = rhs.shape[2]
    sources = conn_src[0, 0]
    place = jnp.take(tile_map, sources)
    peer = place // 2
    slot = place % 2
    live = jnp.arange(sources.shape[0], dtype=jnp.int32) < conn_count[0, 0]
    blocks = areal_blocks[0]
    vert_blocks = vertical_blocks[0]
    rhs_float = rhs[0].astype(jnp.float32)
    lam = rhs
    for step in range(ITERS):
        whole = lax.all_gather(lam, "areal", axis=0, tiled=True)
        chosen = whole[peer, slot]
        chosen = jnp.where(live[:, None, None], chosen, jnp.zeros_like(chosen))
        padded = extended(lam, (("layer", 1),), 1)[0]
        near = jnp.stack([padded[0:2], padded[2:4]], axis=1)
        off = jnp.einsum("sru,dsuv->drv", chosen, blocks, preferred_element_type=jnp.float32)
        off = off + jnp.einsum(
            "dkru,dkuv->drv", near, vert_blocks, preferred_element_type=jnp.float32
        )
        lam = (rhs_float - off).astype(jnp.bfloat16)[None]
    lamf = lam[0].astype(jnp.float32).reshape(2, rows, phases, cells)
    grad = jnp.sum(lamf * sens[0][:, None, :, :], axis=2)
    hits = well_cells[0][:, :, None] == jnp.arange(cells, dtype=jnp.int32)[None, None, :]
    well_sum = jnp.sum(jnp.where(hits, well_gain[0][:, :, None], 0.0), axis=1)
    grad = (grad + well_sum[:, None, :] * lamf[:, :, 0, :]).astype(jnp.bfloat16)
    partial_sum = jnp.einsum("jrc,jcm->rm", grad, basis[0], preferred_element_type=jnp.float32)
    reduced = lax.psum_scatter(partial_sum, "areal", scatter_dimension=1, tiled=True)
    reduced = lax.psum_scatter(reduced, "layer", scatter_dimension=0, tiled=True)
    return (lam, reduced.astype(jnp.bfloat16))


def solution(mesh):
    in_specs = (
        P("areal", "layer", None, None),
        P("areal", "layer", None, None, None),
        P("areal", "layer", None, None, None),
        P("areal", "layer", None),
        P("areal", "layer"),
        P(),
        P("areal", "layer", None),
        P("areal", "layer", None),
        P("areal", "layer", None, None),
        P("areal", "layer", None, None),
    )
    out_specs = (P("areal", "layer", None, None), P("layer", "areal"))
    return jax.shard_map(
        on_device, mesh=mesh, in_specs=in_specs, out_specs=out_specs, check_vma=False
    )
```

profile of v0, /device:TPU:6, one launch (start us, length us, event | category | flops | bytes accessed | tf_op | source)
XLA Modules:
  0.0 398.7 jit_solution(2308188141515170945)
XLA Ops:
  8.0 1.9 fusion.93
  9.9 4.4 %collective-permute-start = (bf16[1,1,112,384]{3,2,1,0:T(8,128)(2,1)}, bf16[1,1,112,384]{3,2,1,0:T(8,128)(2,1)}, u32[]{:S(2)}, u32[]{:S(2)}) collective-permute-start(bf16[1,1,112,384]{3,2,1,0:T(8,128)(2,1)} %get-tuple-element.20), channel_id=1, source_target_pairs={{0,1},{1,2},{2,3},{3,4},{4,5},{5,6},{6,7},{7,8},{8,9},{9,10},{10,1... | collective-permute-start | bytes 258056 | tf_op jit(solution)/shard_map/ppermute | solution.py:16
  18.9 2.1 collective-permute-done.1
  22.0 2.4 convolution_bitcast_fusion.2
  24.4 53.8 %all-gather.6.cloned.1.call-done = bf16[32,2,112,384]{3,2,1,0:T(8,128)(2,1)} async-done(((bf16[1,2,112,384]{3,2,1,0:T(8,128)(2,1)}), bf16[32,2,112,384]{3,2,1,0:T(8,128)(2,1)}) %all-gather.6.cloned.1.call-update) | async-done | bytes 5505040 | tf_op jit(solution)/shard_map/all_gather | solution.py:47
  78.2 4.0 %gather_fusion.1 = bf16[6,112,384]{2,1,0:T(8,128)(2,1)} fusion(bf16[32,2,112,384]{3,2,1,0:T(8,128)(2,1)} %all-gather.6.cloned.1.call-done, s32[6]{0:T(128)S(1)} %fusion.82), kind=kCustom, calls=%fused_computation.1 | custom fusion | bytes 1032240 | tf_op jit(solution)/shard_map/gather | solution.py:48
  82.3 2.5 fusion.33
  85.8 3.5 collective-permute-start.2
  91.5 4.2 %collective-permute-done.3 = bf16[1,1,112,384]{3,2,1,0:T(8,128)(2,1)S(1)} collective-permute-done((bf16[1,1,112,384]{3,2,1,0:T(8,128)(2,1)S(1)}, bf16[1,1,112,384]{3,2,1,0:T(8,128)(2,1)S(1)}, u32[]{:S(2)}, u32[]{:S(2)}) %collective-permute-start.3) | collective-permute-done | bytes 86048 | tf_op jit(solution)/shard_map/ppermute | solution.py:17
  96.7 2.4 convolution_bitcast_fusion.1
  99.0 48.5 %all-gather.8.cloned.1.call-done = bf16[64,112,384]{2,1,0:T(8,128)(2,1)} async-done(((bf16[2,112,384]{2,1,0:T(8,128)(2,1)}), bf16[64,112,384]{2,1,0:T(8,128)(2,1)}) %all-gather.8.cloned.1.call-update) | async-done | bytes 5505040 | tf_op jit(solution)/shard_map/all_gather | solution.py:47
  147.5 4.0 %gather_fusion.2 = bf16[6,112,384]{2,1,0:T(8,128)(2,1)} fusion(bf16[32,2,112,384]{3,2,1,0:T(8,128)(2,1)} %bitcast.157, s32[6]{0:T(128)S(1)} %fusion.82), kind=kCustom, calls=%fused_computation.2 | custom fusion | bytes 1032240 | tf_op jit(solution)/shard_map/gather | solution.py:48
  151.5 2.5 fusion.36
  155.1 3.5 collective-permute-start.4
  160.7 4.2 %collective-permute-done.5 = bf16[1,1,112,384]{3,2,1,0:T(8,128)(2,1)S(1)} collective-permute-done((bf16[1,1,112,384]{3,2,1,0:T(8,128)(2,1)S(1)}, bf16[1,1,112,384]{3,2,1,0:T(8,128)(2,1)S(1)}, u32[]{:S(2)}, u32[]{:S(2)}) %collective-permute-start.5) | collective-permute-done | bytes 86048 | tf_op jit(solution)/shard_map/ppermute | solution.py:17
  165.9 2.4 convolution_bitcast_fusion
  168.3 48.5 %all-gather.10.cloned.1.call-done = bf16[64,112,384]{2,1,0:T(8,128)(2,1)} async-done(((bf16[2,112,384]{2,1,0:T(8,128)(2,1)}), bf16[64,112,384]{2,1,0:T(8,128)(2,1)}) %all-gather.10.cloned.1.call-update) | async-done | bytes 5505040 | tf_op jit(solution)/shard_map/all_gather | solution.py:47
  216.8 4.0 %gather_fusion.3 = bf16[6,112,384]{2,1,0:T(8,128)(2,1)} fusion(bf16[32,2,112,384]{3,2,1,0:T(8,128)(2,1)} %bitcast.156, s32[6]{0:T(128)S(1)} %fusion.82), kind=kCustom, calls=%fused_computation.3 | custom fusion | bytes 1032240 | tf_op jit(solution)/shard_map/gather | solution.py:48
  220.8 2.5 fusion.39
  223.3 1.8 copy.34
  226.3 1.9 convolution_bitcast_fusion.3
  228.2 1.3 dynamic-slice.2
  232.1 127.4 %all-reduce.4.cloned.1.call-done = f32[112,256]{0,1:T(8,128)} async-done(((f32[112,256]{0,1:T(8,128)}), f32[112,256]{0,1:T(8,128)}) %all-reduce.4.cloned.1.call-update) | async-done | bytes 114704
  360.2 31.3 %all-reduce.1 = bf16[112,8]{0,1:T(8,128)(2,1)S(1)} all-reduce(f32[112,8]{0,1:T(8,128)S(1)} %constant_dynamic-slice_fusion), channel_id=5, replica_groups=mesh['areal'=32,'layer'=16] {'layer'}, use_global_device_ids=true, to_apply=%region_3.4.clone | all-reduce | flops 896 | bytes 5376
  (35 shorter events, 17.9 us)
Async XLA Ops:
  7.2 75.1 %copy-start = (bf16[1,2,6,384,384]{4,3,2,1,0:T(8,128)(2,1)S(1)}, bf16[1,2,6,384,384]{4,3,2,1,0:T(8,128)(2,1)}, u32[]{:S(2)}) copy-start(bf16[1,2,6,384,384]{4,3,2,1,0:T(8,128)(2,1)} %param.11) | copy-start | bytes 10616836
  7.2 71.1 %all-gather.6.cloned.1.call-start = ((), (), s32[]{:S(2)}) async-start(), calls=%async_computation | async-start | bytes 5677056 | tf_op jit(solution)/shard_map/all_gather | solution.py:47
  7.9 139.6 %all-gather.8.cloned.1.call-start = ((), (), s32[]{:S(2)}) async-start(), calls=%async_computation.1 | async-start | bytes 5677056 | tf_op jit(solution)/shard_map/all_gather | solution.py:47
  9.9 9.0 %collective-permute-start = (bf16[1,1,112,384]{3,2,1,0:T(8,128)(2,1)}, bf16[1,1,112,384]{3,2,1,0:T(8,128)(2,1)}, u32[]{:S(2)}, u32[]{:S(2)}) collective-permute-start(bf16[1,1,112,384]{3,2,1,0:T(8,128)(2,1)} %get-tuple-element.20), channel_id=1, source_target_pairs={{0,1},{1,2},{2,3},{3,4},{4,5},{5,6},{6,7},{7,8},{8,9},{9,10},{10,1... | collective-permute-start | bytes 258056 | tf_op jit(solution)/shard_map/ppermute | solution.py:16
  14.3 6.7 %collective-permute-start.1 = (bf16[1,1,112,384]{3,2,1,0:T(8,128)(2,1)}, bf16[1,1,112,384]{3,2,1,0:T(8,128)(2,1)}, u32[]{:S(2)}, u32[]{:S(2)}) collective-permute-start(bf16[1,1,112,384]{3,2,1,0:T(8,128)(2,1)} %get-tuple-element.21), channel_id=1, source_target_pairs={{1,0},{2,1},{3,2},{4,3},{5,4},{6,5},{7,6},{8,7},{9,8},{10,9},{11,1... | collective-permute-start | bytes 258056 | tf_op jit(solution)/shard_map/ppermute | solution.py:17
  84.8 131.9 %all-gather.10.cloned.1.call-start = ((), (), s32[]{:S(2)}) async-start(), calls=%async_computation.2 | async-start | bytes 5677056 | tf_op jit(solution)/shard_map/all_gather | solution.py:47
  85.8 5.6 %collective-permute-start.2 = (bf16[1,1,112,384]{3,2,1,0:T(8,128)(2,1)S(1)}, bf16[1,1,112,384]{3,2,1,0:T(8,128)(2,1)S(1)}, u32[]{:S(2)}, u32[]{:S(2)}) collective-permute-start(bf16[1,1,112,384]{3,2,1,0:T(8,128)(2,1)S(1)} %get-tuple-element.16), channel_id=1, source_target_pairs={{0,1},{1,2},{2,3},{3,4},{4,5},{5,6},{6,7},{7,8},{8,9},{9,10},{10,1... | collective-permute-start | bytes 258056 | tf_op jit(solution)/shard_map/ppermute | solution.py:16
  89.3 6.4 %collective-permute-start.3 = (bf16[1,1,112,384]{3,2,1,0:T(8,128)(2,1)S(1)}, bf16[1,1,112,384]{3,2,1,0:T(8,128)(2,1)S(1)}, u32[]{:S(2)}, u32[]{:S(2)}) collective-permute-start(bf16[1,1,112,384]{3,2,1,0:T(8,128)(2,1)S(1)} %get-tuple-element.17), channel_id=1, source_target_pairs={{1,0},{2,1},{3,2},{4,3},{5,4},{6,5},{7,6},{8,7},{9,8},{10,9},{11,1... | collective-permute-start | bytes 258056 | tf_op jit(solution)/shard_map/ppermute | solution.py:17
  96.7 57.5 %copy-start.1 = (f32[1,2,3,128]{3,1,2,0:T(2,128)S(1)}, f32[1,2,3,128]{3,1,2,0:T(2,128)}, u32[]{:S(2)}) copy-start(f32[1,2,3,128]{3,1,2,0:T(2,128)} %param.18) | copy-start | bytes 9220
  154.1 205.4 %all-reduce.4.cloned.1.call-start = ((), (), s32[]{:S(2)}) async-start(), calls=%async_computation.3 | async-start | bytes 262144
  155.1 5.6 %collective-permute-start.4 = (bf16[1,1,112,384]{3,2,1,0:T(8,128)(2,1)S(1)}, bf16[1,1,112,384]{3,2,1,0:T(8,128)(2,1)S(1)}, u32[]{:S(2)}, u32[]{:S(2)}) collective-permute-start(bf16[1,1,112,384]{3,2,1,0:T(8,128)(2,1)S(1)} %get-tuple-element.12), channel_id=1, source_target_pairs={{0,1},{1,2},{2,3},{3,4},{4,5},{5,6},{6,7},{7,8},{8,9},{9,10},{10,1... | collective-permute-start | bytes 258056 | tf_op jit(solution)/shard_map/ppermute | solution.py:16
  158.6 6.4 %collective-permute-start.5 = (bf16[1,1,112,384]{3,2,1,0:T(8,128)(2,1)S(1)}, bf16[1,1,112,384]{3,2,1,0:T(8,128)(2,1)S(1)}, u32[]{:S(2)}, u32[]{:S(2)}) collective-permute-start(bf16[1,1,112,384]{3,2,1,0:T(8,128)(2,1)S(1)} %get-tuple-element.13), channel_id=1, source_target_pairs={{1,0},{2,1},{3,2},{4,3},{5,4},{6,5},{7,6},{8,7},{9,8},{10,9},{11,1... | collective-permute-start | bytes 258056 | tf_op jit(solution)/shard_map/ppermute | solution.py:17
Sparse Core Ops, SparseCore 0:
  11.1 67.0 all-gather.5
  84.9 62.5 all-gather.7
  154.2 62.5 all-gather.9
  228.3 131.1 all-reduce.3
where the time goes:
time: 400 us; the launch traced here: 399 us
  waiting for transfers between devices  290 us (72%)
  blocking collectives  31.3 us (8%)
  local copies, waits for them, and re-layouts  22.9 us (6%)
  matrix products  16.6 us (4%)
  between operations  15.8 us (4%)
  starting transfers between devices  15.4 us (4%)
  other arithmetic  6.32 us (2%)
    all_gather x3, waiting for transfers between devices, on_device(): whole = lax.all_gather(lam, 'areal', axis=0, tiled=True)  151 us
    unnamed x5, waiting for transfers between devices  128 us
    unnamed x1, blocking collectives  31.3 us
    gather x3, local copies, waits for them, and re-layouts, on_device(): chosen = whole[peer, slot]  12 us
    ppermute x3, starting transfers between devices, extended(): before = lax.ppermute(last, axis, up)  11.4 us
    ppermute x3, waiting for transfers between devices, extended(): after = lax.ppermute(leading, axis, down)  10.5 us
  transfers between devices with their start and end apart: 10, of which 9 were waited for; matrix products, arithmetic and copies ran while one was open for 5% of the time, Pallas kernels for 0%

commit v1 on v0

--- a/solution.py
+++ b/solution.py
@@ -44,7 +44,9 @@
     rhs_float = rhs[0].astype(jnp.float32)
     lam = rhs
     for step in range(ITERS):
-        whole = lax.all_gather(lam, "areal", axis=0, tiled=True)
+        whole = jnp.concatenate(
+            lax.all_to_all(jnp.stack([lam] * lax.axis_size("areal")), "areal", 0, 0), axis=0
+        )
         chosen = whole[peer, slot]
         chosen = jnp.where(live[:, None, None], chosen, jnp.zeros_like(chosen))
         padded = extended(lam, (("layer", 1),), 1)[0]

time: 400 us -> 437 us (1.093)
  starting transfers between devices: 15.4 us -> 37.3 us
  local copies, waits for them, and re-layouts: 22.9 us -> 33.2 us
  waiting for transfers between devices: 290 us -> 298 us
    all_to_all x0 -> x3, waiting for transfers between devices: none -> 155 us  [on_device(): lax.all_to_all(jnp.stack([lam] * lax.axis_size('areal')), 'areal', 0, 0)]
    all_gather x3 -> x0, waiting for transfers between devices: 151 us -> none  [on_device(): whole = lax.all_gather(lam, 'areal', axis=0, tiled=True)]
    all_to_all x0 -> x3, starting transfers between devices: none -> 28.9 us  [on_device(): lax.all_to_all(jnp.stack([lam] * lax.axis_size('areal')), 'areal', 0, 0)]
    another operation x0 -> x3, local copies, waits for them, and re-layouts: none -> 9.83 us  [on_device(): jnp.stack([lam] * lax.axis_size('areal'))]
    ppermute x3, starting transfers between devices: 11.4 us -> 4.51 us  [extended(): before = lax.ppermute(last, axis, up)]
    unnamed x5 -> x2, waiting for transfers between devices: 128 us -> 129 us
  transfers between devices with their start and end apart: 10 -> 10, of which waited for: 9 -> 9; matrix products, arithmetic and copies ran while one was open for 5% -> 4% of each run, Pallas kernels for 0% -> 0%
where the time goes in v1:
time: 437 us; the launch traced here: 436 us
  waiting for transfers between devices  298 us (68%)
  starting transfers between devices  37.3 us (9%)
  local copies, waits for them, and re-layouts  33.2 us (8%)
  blocking collectives  31.3 us (7%)
  between operations  16.2 us (4%)
  matrix products  15.3 us (4%)
  other arithmetic  5 us (1%)
    all_to_all x3, waiting for transfers between devices, on_device(): lax.all_to_all(jnp.stack([lam] * lax.axis_size('areal')), 'areal', 0, 0)  155 us
    unnamed x2, waiting for transfers between devices  129 us
    unnamed x1, blocking collectives  31.3 us
    all_to_all x3, starting transfers between devices, on_device(): lax.all_to_all(jnp.stack([lam] * lax.axis_size('areal')), 'areal', 0, 0)  28.9 us
    ppermute x3, waiting for transfers between devices, extended(): after = lax.ppermute(leading, axis, down)  12.3 us
    gather x3, local copies, waits for them, and re-layouts, on_device(): chosen = whole[peer, slot]  12 us
    another operation x3, local copies, waits for them, and re-layouts, on_device(): jnp.stack([lam] * lax.axis_size('areal'))  9.83 us
  transfers between devices with their start and end apart: 10, of which 9 were waited for; matrix products, arithmetic and copies ran while one was open for 4% of the time, Pallas kernels for 0%

profile of v1, /device:TPU:6, one launch (start us, length us, event | category | flops | bytes accessed | tf_op | source)
XLA Modules:
  0.0 436.0 jit_solution(6290745087045806727)
XLA Ops:
  7.2 4.0 stack.24
  11.2 10.5 %all-to-all-start = ((bf16[32,1,2,112,384]{4,3,2,1,0:T(8,128)(2,1)}), bf16[32,1,2,112,384]{4,3,2,1,0:T(8,128)(2,1)}, u32[]{:S(2)}, u32[]{:S(2)}) async-start(bf16[32,1,2,112,384]{4,3,2,1,0:T(8,128)(2,1)} %stack.24), calls=%async_computation | async-start | bytes 11010048 | tf_op jit(solution)/shard_map/all_to_all | solution.py:48
  23.3 1.9 collective-permute-start
  27.9 4.1 collective-permute-done.1
  33.0 2.4 convolution_bitcast_fusion.2
  35.4 50.7 %all-to-all-done = bf16[32,1,2,112,384]{4,3,2,1,0:T(8,128)(2,1)} async-done(((bf16[32,1,2,112,384]{4,3,2,1,0:T(8,128)(2,1)}), bf16[32,1,2,112,384]{4,3,2,1,0:T(8,128)(2,1)}, u32[]{:S(2)}, u32[]{:S(2)}) %all-to-all-start) | async-done | bytes 5505056 | tf_op jit(solution)/shard_map/all_to_all | solution.py:48
  86.1 4.0 gather_fusion.1
  90.2 1.9 fusion.33
  92.7 2.9 stack.28
  95.6 9.2 %all-to-all-start.1 = ((bf16[32,1,2,112,384]{4,3,2,1,0:T(8,128)(2,1)}), bf16[32,1,2,112,384]{4,3,2,1,0:T(8,128)(2,1)}, u32[]{:S(2)}, u32[]{:S(2)}) async-start(bf16[32,1,2,112,384]{4,3,2,1,0:T(8,128)(2,1)} %stack.28), calls=%async_computation.1 | async-start | bytes 11010048 | tf_op jit(solution)/shard_map/all_to_all | solution.py:48
  109.4 4.1 collective-permute-done.3
  114.5 2.4 convolution_bitcast_fusion.1
  116.9 52.4 %all-to-all-done.1 = bf16[32,1,2,112,384]{4,3,2,1,0:T(8,128)(2,1)} async-done(((bf16[32,1,2,112,384]{4,3,2,1,0:T(8,128)(2,1)}), bf16[32,1,2,112,384]{4,3,2,1,0:T(8,128)(2,1)}, u32[]{:S(2)}, u32[]{:S(2)}) %all-to-all-start.1) | async-done | bytes 5505056 | tf_op jit(solution)/shard_map/all_to_all | solution.py:48
  169.3 4.0 gather_fusion.2
  175.8 2.9 stack.32
  178.7 9.3 %all-to-all-start.2 = ((bf16[32,1,2,112,384]{4,3,2,1,0:T(8,128)(2,1)}), bf16[32,1,2,112,384]{4,3,2,1,0:T(8,128)(2,1)}, u32[]{:S(2)}, u32[]{:S(2)}) async-start(bf16[32,1,2,112,384]{4,3,2,1,0:T(8,128)(2,1)} %stack.32), calls=%async_computation.2 | async-start | bytes 11010048 | tf_op jit(solution)/shard_map/all_to_all | solution.py:48
  192.7 4.1 collective-permute-done.5
  197.8 2.4 convolution_bitcast_fusion
  200.2 52.3 %all-to-all-done.2 = bf16[32,1,2,112,384]{4,3,2,1,0:T(8,128)(2,1)} async-done(((bf16[32,1,2,112,384]{4,3,2,1,0:T(8,128)(2,1)}), bf16[32,1,2,112,384]{4,3,2,1,0:T(8,128)(2,1)}, u32[]{:S(2)}, u32[]{:S(2)}) %all-to-all-start.2) | async-done | bytes 5505056 | tf_op jit(solution)/shard_map/all_to_all | solution.py:48
  252.5 4.0 gather_fusion.3
  256.5 2.5 fusion.39
  262.0 1.9 convolution_bitcast_fusion.3
  267.8 128.7 %all-reduce.4.cloned.1.call-done = f32[112,256]{0,1:T(8,128)} async-done(((f32[112,256]{0,1:T(8,128)}), f32[112,256]{0,1:T(8,128)}) %all-reduce.4.cloned.1.call-update) | async-done | bytes 114704
  397.2 31.3 %all-reduce.1 = bf16[112,8]{0,1:T(8,128)(2,1)S(1)} all-reduce(f32[112,8]{0,1:T(8,128)S(1)} %constant_dynamic-slice_fusion), channel_id=3, replica_groups=mesh['areal'=32,'layer'=16] {'layer'}, use_global_device_ids=true, to_apply=%region_3.4.clone | all-reduce | flops 896 | bytes 5376
  (43 shorter events, 26.0 us)
Async XLA Ops:
  7.2 83.0 %copy-start = (bf16[1,2,6,384,384]{4,3,2,1,0:T(8,128)(2,1)S(1)}, bf16[1,2,6,384,384]{4,3,2,1,0:T(8,128)(2,1)}, u32[]{:S(2)}) copy-start(bf16[1,2,6,384,384]{4,3,2,1,0:T(8,128)(2,1)} %param.11) | copy-start | bytes 10616836
  11.2 16.0 %copy-start.5 = (s32[1,1,6]{2,1,0:T(1,128)S(1)}, s32[1,1,6]{2,1,0:T(1,128)}, u32[]{:S(2)}) copy-start(s32[1,1,6]{2,1,0:T(1,128)} %param.13) | copy-start | bytes 76
  11.2 16.0 %copy-start.1 = (s32[64]{0:T(128)S(1)}, s32[64]{0:T(128)}, u32[]{:S(2)}) copy-start(s32[64]{0:T(128)} %param.15) | copy-start | bytes 772
  11.2 75.0 %all-to-all-start = ((bf16[32,1,2,112,384]{4,3,2,1,0:T(8,128)(2,1)}), bf16[32,1,2,112,384]{4,3,2,1,0:T(8,128)(2,1)}, u32[]{:S(2)}, u32[]{:S(2)}) async-start(bf16[32,1,2,112,384]{4,3,2,1,0:T(8,128)(2,1)} %stack.24), calls=%async_computation | async-start | bytes 11010048 | tf_op jit(solution)/shard_map/all_to_all | solution.py:48
  23.3 4.6 %collective-permute-start = (bf16[1,1,112,384]{3,2,1,0:T(8,128)(2,1)}, bf16[1,1,112,384]{3,2,1,0:T(8,128)(2,1)}, u32[]{:S(2)}, u32[]{:S(2)}) collective-permute-start(bf16[1,1,112,384]{3,2,1,0:T(8,128)(2,1)} %get-tuple-element.20), channel_id=1, source_target_pairs={{0,1},{1,2},{2,3},{3,4},{4,5},{5,6},{6,7},{7,8},{8,9},{9,10},{10,1... | collective-permute-start | bytes 258056 | tf_op jit(solution)/shard_map/ppermute | solution.py:16
  25.2 6.8 %collective-permute-start.1 = (bf16[1,1,112,384]{3,2,1,0:T(8,128)(2,1)}, bf16[1,1,112,384]{3,2,1,0:T(8,128)(2,1)}, u32[]{:S(2)}, u32[]{:S(2)}) collective-permute-start(bf16[1,1,112,384]{3,2,1,0:T(8,128)(2,1)} %get-tuple-element.21), channel_id=1, source_target_pairs={{1,0},{2,1},{3,2},{4,3},{5,4},{6,5},{7,6},{8,7},{9,8},{10,9},{11,1... | collective-permute-start | bytes 258056 | tf_op jit(solution)/shard_map/ppermute | solution.py:17
  92.0 0.7 copy-start.3
  95.6 73.6 %all-to-all-start.1 = ((bf16[32,1,2,112,384]{4,3,2,1,0:T(8,128)(2,1)}), bf16[32,1,2,112,384]{4,3,2,1,0:T(8,128)(2,1)}, u32[]{:S(2)}, u32[]{:S(2)}) async-start(bf16[32,1,2,112,384]{4,3,2,1,0:T(8,128)(2,1)} %stack.28), calls=%async_computation.1 | async-start | bytes 11010048 | tf_op jit(solution)/shard_map/all_to_all | solution.py:48
  105.7 3.7 collective-permute-start.2
  107.0 6.5 %collective-permute-start.3 = (bf16[1,1,112,384]{3,2,1,0:T(8,128)(2,1)S(1)}, bf16[1,1,112,384]{3,2,1,0:T(8,128)(2,1)S(1)}, u32[]{:S(2)}, u32[]{:S(2)}) collective-permute-start(bf16[1,1,112,384]{3,2,1,0:T(8,128)(2,1)S(1)} %get-tuple-element.17), channel_id=1, source_target_pairs={{1,0},{2,1},{3,2},{4,3},{5,4},{6,5},{7,6},{8,7},{9,8},{10,9},{11,1... | collective-permute-start | bytes 258056 | tf_op jit(solution)/shard_map/ppermute | solution.py:17
  175.1 0.7 copy-start.2
  178.7 9.3 %copy-start.4 = (f32[1,2,3,128]{3,1,2,0:T(2,128)S(1)}, f32[1,2,3,128]{3,1,2,0:T(2,128)}, u32[]{:S(2)}) copy-start(f32[1,2,3,128]{3,1,2,0:T(2,128)} %param.18) | copy-start | bytes 9220
  178.7 73.8 %all-to-all-start.2 = ((bf16[32,1,2,112,384]{4,3,2,1,0:T(8,128)(2,1)}), bf16[32,1,2,112,384]{4,3,2,1,0:T(8,128)(2,1)}, u32[]{:S(2)}, u32[]{:S(2)}) async-start(bf16[32,1,2,112,384]{4,3,2,1,0:T(8,128)(2,1)} %stack.32), calls=%async_computation.2 | async-start | bytes 11010048 | tf_op jit(solution)/shard_map/all_to_all | solution.py:48
  188.0 208.5 %all-reduce.4.cloned.1.call-start = ((), (), s32[]{:S(2)}) async-start(), calls=%async_computation.3 | async-start | bytes 262144
  189.1 3.7 collective-permute-start.4
  190.4 6.5 %collective-permute-start.5 = (bf16[1,1,112,384]{3,2,1,0:T(8,128)(2,1)S(1)}, bf16[1,1,112,384]{3,2,1,0:T(8,128)(2,1)S(1)}, u32[]{:S(2)}, u32[]{:S(2)}) collective-permute-start(bf16[1,1,112,384]{3,2,1,0:T(8,128)(2,1)S(1)} %get-tuple-element.13), channel_id=1, source_target_pairs={{1,0},{2,1},{3,2},{4,3},{5,4},{6,5},{7,6},{8,7},{9,8},{10,9},{11,1... | collective-permute-start | bytes 258056 | tf_op jit(solution)/shard_map/ppermute | solution.py:17
Sparse Core Ops, SparseCore 0:
  264.1 132.3 all-reduce.3
